TPU v7x, 256 devices: a whole 4x4x8 slice. The times are simulated.
256 devices in a mesh: ctx: 64 (over y_hi, x, z), fsdp: 4 (over y_lo, core).
Axes of the slice: x: 4, y: 4 (y_hi: 2, y_lo: 2; y = y_hi * 2 + y_lo), z: 8, core: 2. Of those that a mesh axis runs over, the one named last changes fastest.
Arguments:
- tokens: bfloat16 [1048576, 512], P('ctx', 'fsdp'), may hold values from -6 to 6
- factor_d: bfloat16 [32768, 32, 32], P(('ctx', 'fsdp')), may hold values from -1 to 1
- factor_c: bfloat16 [32768, 32, 32], P(('ctx', 'fsdp')), may hold values from -1 to 1
- factor_b: bfloat16 [32768, 32, 32], P(('ctx', 'fsdp')), may hold values from -1 to 1
- factor_a: bfloat16 [32768, 32, 32], P(('ctx', 'fsdp')), may hold values from -1 to 1
- w_proj: bfloat16 [512, 512], P(None, 'fsdp'), may hold values from -0.25 to 0.25
Outputs:
- output: bfloat16 [1048576, 512], P('ctx', 'fsdp')
All inputs are finite; a program needn't handle non-finite values.
Results may differ from a plain program's by a relative error of at most 0.0076.
Values may be sent and summed in bfloat16 or wider, within the bound.
No kernel may reach another device: no remote copies, remote signals or barrier semaphores. Data moves between devices by JAX's collectives and lax.ppermute only.
A program may use at most 128 MiB of HBM per device.

v0:
```python
import jax
import jax.numpy as jnp
from jax import lax
from jax.sharding import PartitionSpec as P


def body(tokens, factor_d, factor_c, factor_b, factor_a, w_proj):
    ctx_count = lax.axis_size("ctx")
    local_rows, channels = tokens.shape
    block_size = factor_d.shape[1]
    group_size = block_size * block_size // ctx_count
    blocks_first, blocks_second, blocks_third, blocks_last = (
        lax.all_gather(factor_d, "fsdp", axis=0, tiled=True),
        lax.all_gather(factor_c, "fsdp", axis=0, tiled=True),
        lax.all_gather(factor_b, "fsdp", axis=0, tiled=True),
        lax.all_gather(factor_a, "fsdp", axis=0, tiled=True),
    )
    first = jnp.einsum(
        "gij,gjc->gic",
        blocks_first,
        tokens.reshape(-1, block_size, channels),
        preferred_element_type=jnp.float32,
    ).astype(jnp.bfloat16)
    weights_c = blocks_second.reshape(group_size, block_size, block_size, block_size)
    second = jnp.einsum(
        "pdij,pjdc->pidc",
        weights_c,
        first.reshape(group_size, block_size, block_size, channels),
        preferred_element_type=jnp.float32,
    ).astype(jnp.bfloat16)
    sectioned = second.reshape(group_size, ctx_count, group_size, channels)
    weights_b = blocks_third.reshape(group_size, block_size, block_size, block_size)
    weights_a = blocks_last.reshape(group_size, block_size, block_size, block_size)
    part = lax.all_to_all(sectioned, "ctx", split_axis=1, concat_axis=0, tiled=True)
    width = part.shape[3]
    held = part.reshape(block_size, block_size, group_size, width)
    third = jnp.einsum(
        "laij,ajlc->ailc", weights_b, held, preferred_element_type=jnp.float32
    ).astype(jnp.bfloat16)
    fourth = jnp.einsum(
        "lbij,jblc->iblc", weights_a, third, preferred_element_type=jnp.float32
    ).astype(jnp.bfloat16)
    outgoing = fourth.reshape(block_size * block_size, 1, group_size, width)
    mixed = lax.all_to_all(outgoing, "ctx", split_axis=0, concat_axis=1, tiled=True).reshape(
        local_rows, channels
    )
    gated = (mixed.astype(jnp.float32) * jax.nn.silu(tokens.astype(jnp.float32))).astype(
        jnp.bfloat16
    )
    summed = jnp.dot(
        lax.all_gather(gated, "fsdp", axis=1, tiled=True),
        w_proj,
        preferred_element_type=jnp.float32,
    )
    return summed.astype(jnp.bfloat16)


def solution(mesh):
    in_specs = (
        P("ctx", "fsdp"),
        P(("ctx", "fsdp"), None, None),
        P(("ctx", "fsdp"), None, None),
        P(("ctx", "fsdp"), None, None),
        P(("ctx", "fsdp"), None, None),
        P(None, "fsdp"),
    )
    out_specs = P("ctx", "fsdp")
    return jax.shard_map(body, mesh=mesh, in_specs=in_specs, out_specs=out_specs, check_vma=False)
```

profile of v0, /device:TPU:1, one launch (start us, length us, event | category | flops | bytes accessed | tf_op | source)
XLA Modules:
  0.0 481.7 jit_solution(16337362832562375488)
XLA Ops:
  6.5 0.0 copy-start
  6.5 0.0 all-gather.6.cloned.1.call-start
  6.5 0.7 all-gather.6.cloned.1.call-update
  7.3 0.0 all-gather.8.cloned.1.call-start
  7.3 0.7 all-gather.8.cloned.1.call-update
  8.0 28.3 %all-gather.6.cloned.1.call-done = bf16[512,32,32]{0,2,1:T(8,128)(2,1)} async-done(((bf16[128,32,32]{0,2,1:T(8,128)(2,1)}), bf16[512,32,32]{0,2,1:T(8,128)(2,1)}) %all-gather.6.cloned.1.call-update) | async-done | bytes 1048592 | tf_op jit(solution)/shard_map/all_gather | solution.py:13
  36.3 7.2 %copy.38 = bf16[512,32,32]{2,1,0:T(8,128)(2,1)} copy(bf16[512,32,32]{0,2,1:T(8,128)(2,1)} %all-gather.6.cloned.1.call-done) | data formatting | bytes 2097152 | tf_op jit(solution)/shard_map/all_gather | solution.py:13
  43.5 6.7 %convolution_convert_fusion.1 = bf16[512,32,128]{2,1,0:T(8,128)(2,1)} fusion(bf16[512,32,32]{2,1,0:T(8,128)(2,1)} %copy.38, bf16[512,32,128]{2,1,0:T(8,128)(2,1)} %bitcast.42), kind=kOutput, calls=%fused_computation.18 | convolution fusion | flops 136314880 | bytes 9437184 | tf_op jit(solution)/shard_map/gij,gjc->gic/dot_general | solution.py:18
  50.2 12.7 %all-gather.8.cloned.1.call-done = bf16[512,32,32]{0,2,1:T(8,128)(2,1)} async-done(((bf16[128,32,32]{0,2,1:T(8,128)(2,1)}), bf16[512,32,32]{0,2,1:T(8,128)(2,1)}) %all-gather.8.cloned.1.call-update) | async-done | bytes 1048592 | tf_op jit(solution)/shard_map/all_gather | solution.py:14
  62.9 7.2 %copy.39 = bf16[512,32,32]{2,1,0:T(8,128)(2,1)} copy(bf16[512,32,32]{0,2,1:T(8,128)(2,1)} %all-gather.8.cloned.1.call-done) | data formatting | bytes 2097152 | tf_op jit(solution)/shard_map/all_gather | solution.py:14
  70.1 5.1 %convert_bitcast_fusion.3 = bf16[16,32,32,128]{3,1,2,0:T(8,128)(2,1)S(1)} fusion(bf16[16,32,32,32]{3,2,1,0:T(8,128)(2,1)} %bitcast.40, bf16[16,32,32,128]{3,2,1,0:T(8,128)(2,1)} %bitcast.39), kind=kOutput, calls=%fused_computation.17 | convolution fusion | flops 136314880 | bytes 9437184 | tf_op jit(solution)/shard_map/pdij,pjdc->pidc/dot_general | solution.py:25
  75.1 1.8 copy.41
  76.9 3.2 copy.42
  80.1 13.4 %all-to-all-start = ((bf16[16,64,16,128]{3,2,0,1:T(8,128)(2,1)}), bf16[16,64,16,128]{3,2,0,1:T(8,128)(2,1)}, u32[]{:S(2)}, u32[]{:S(2)}) async-start(bf16[16,64,16,128]{3,2,0,1:T(8,128)(2,1)} %copy.42), calls=%async_computation | async-start | bytes 8388608 | tf_op jit(solution)/shard_map/all_to_all | solution.py:34
  93.5 0.0 all-gather.12.cloned.1.call-start
  93.6 0.7 all-gather.12.cloned.1.call-update
  94.3 0.0 all-gather.10.cloned.1.call-start
  94.3 0.5 all-gather.10.cloned.1.call-update
  94.9 0.2 all-gather.14.cloned.1.call-start
  95.1 31.2 %all-gather.12.cloned.1.call-done = bf16[512,32,32]{0,2,1:T(8,128)(2,1)} async-done(((bf16[128,32,32]{0,2,1:T(8,128)(2,1)}), bf16[512,32,32]{0,2,1:T(8,128)(2,1)}) %all-gather.12.cloned.1.call-update) | async-done | bytes 1048592 | tf_op jit(solution)/shard_map/all_gather | solution.py:16
  126.3 5.9 %reshape.37 = bf16[16,32,32,32]{1,0,3,2:T(8,128)(2,1)} reshape(bf16[512,32,32]{0,2,1:T(8,128)(2,1)} %all-gather.12.cloned.1.call-done) | data formatting | bytes 2097152 | tf_op jit(solution)/shard_map/reshape | solution.py:33
  132.2 10.3 %copy.46 = bf16[16,32,32,32]{3,2,0,1:T(8,128)(2,1)} copy(bf16[16,32,32,32]{1,0,3,2:T(8,128)(2,1)} %reshape.37) | data formatting | bytes 2097152 | tf_op jit(solution)/shard_map/reshape | solution.py:33
  142.6 21.9 %all-gather.10.cloned.1.call-done = bf16[512,32,32]{0,2,1:T(8,128)(2,1)} async-done(((bf16[128,32,32]{0,2,1:T(8,128)(2,1)}), bf16[512,32,32]{0,2,1:T(8,128)(2,1)}) %all-gather.10.cloned.1.call-update) | async-done | bytes 1048592 | tf_op jit(solution)/shard_map/all_gather | solution.py:15
  164.5 5.9 %reshape.36 = bf16[16,32,32,32]{1,0,3,2:T(8,128)(2,1)} reshape(bf16[512,32,32]{0,2,1:T(8,128)(2,1)} %all-gather.10.cloned.1.call-done) | data formatting | bytes 2097152 | tf_op jit(solution)/shard_map/reshape | solution.py:32
  170.4 10.4 %copy.44 = bf16[16,32,32,32]{3,2,0,1:T(8,128)(2,1)} copy(bf16[16,32,32,32]{1,0,3,2:T(8,128)(2,1)} %reshape.36) | data formatting | bytes 2097152 | tf_op jit(solution)/shard_map/reshape | solution.py:32
  180.8 5.6 %all-to-all-done = bf16[16,64,16,128]{3,2,0,1:T(8,128)(2,1)} async-done(((bf16[16,64,16,128]{3,2,0,1:T(8,128)(2,1)}), bf16[16,64,16,128]{3,2,0,1:T(8,128)(2,1)}, u32[]{:S(2)}, u32[]{:S(2)}) %all-to-all-start) | async-done | bytes 4194336 | tf_op jit(solution)/shard_map/all_to_all | solution.py:34
  186.4 0.0 copy-start.1
  186.4 4.8 %convert_bitcast_fusion.2 = bf16[32,32,16,128]{3,1,2,0:T(8,128)(2,1)S(1)} fusion(bf16[16,32,32,32]{3,2,0,1:T(8,128)(2,1)} %copy.44, bf16[32,32,16,128]{3,2,1,0:T(8,128)(2,1)} %bitcast.7), kind=kOutput, calls=%fused_computation.16 | convolution fusion | flops 136314880 | bytes 9437184 | tf_op jit(solution)/shard_map/laij,ajlc->ailc/dot_general | solution.py:37
  191.2 0.0 copy-done.1
  191.2 4.7 convert_bitcast_fusion.1
  196.0 1.6 copy.47
  197.6 105.4 %all_to_all.24 = bf16[1024,1,16,128]{3,2,1,0:T(8,128)(2,1)S(1)} all-to-all(bf16[1024,1,16,128]{3,2,1,0:T(8,128)(2,1)S(1)} %bitcast.44), channel_id=1, replica_groups=mesh['ctx'=64,'fsdp'=4] {'ctx'}, dimensions={0} | all-to-all | bytes 8388608 | tf_op jit(solution)/shard_map/all_to_all | solution.py:44
  303.0 1.1 convert_bitcast_fusion
  304.1 0.0 copy-start.2
  304.1 0.9 copy.50
  305.0 1.3 copy-done.2
  306.3 4.1 fusion.4
  310.4 0.0 all-gather.14.cloned.1.call-update
  310.4 152.4 %all-gather.14.cloned.1.call-done = bf16[16384,512]{1,0:T(8,128)(2,1)} async-done(((bf16[16384,128]{1,0:T(8,128)(2,1)}), bf16[16384,512]{1,0:T(8,128)(2,1)}) %all-gather.14.cloned.1.call-update) | async-done | bytes 16777232 | tf_op jit(solution)/shard_map/all_gather | solution.py:51
  462.9 0.0 copy-done
  462.9 12.3 %convolution_convert_fusion = bf16[16384,128]{1,0:T(8,128)(2,1)} fusion(bf16[16384,512]{1,0:T(8,128)(2,1)} %all-gather.14.cloned.1.call-done, bf16[512,128]{1,0:T(8,128)(2,1)S(1)} %copy-done), kind=kOutput, calls=%fused_computation | convolution fusion | flops 2149580800 | bytes 21102592 | tf_op jit(solution)/shard_map/dot_general | solution.py:50
Async XLA Ops:
  6.5 456.3 %copy-start = (bf16[512,128]{1,0:T(8,128)(2,1)S(1)}, bf16[512,128]{1,0:T(8,128)(2,1)}, u32[]{:S(2)}) copy-start(bf16[512,128]{1,0:T(8,128)(2,1)} %param.11) | copy-start | bytes 393220
  6.5 29.8 %all-gather.6.cloned.1.call-start = ((), (), s32[]{:S(2)}) async-start(), calls=%async_computation.2 | async-start | bytes 1310720 | tf_op jit(solution)/shard_map/all_gather | solution.py:13
  7.3 55.6 %all-gather.8.cloned.1.call-start = ((), (), s32[]{:S(2)}) async-start(), calls=%async_computation.3 | async-start | bytes 1310720 | tf_op jit(solution)/shard_map/all_gather | solution.py:14
  80.1 106.3 %all-to-all-start = ((bf16[16,64,16,128]{3,2,0,1:T(8,128)(2,1)}), bf16[16,64,16,128]{3,2,0,1:T(8,128)(2,1)}, u32[]{:S(2)}, u32[]{:S(2)}) async-start(bf16[16,64,16,128]{3,2,0,1:T(8,128)(2,1)} %copy.42), calls=%async_computation | async-start | bytes 8388608 | tf_op jit(solution)/shard_map/all_to_all | solution.py:34
  93.5 32.8 %all-gather.12.cloned.1.call-start = ((), (), s32[]{:S(2)}) async-start(), calls=%async_computation.5 | async-start | bytes 1310720 | tf_op jit(solution)/shard_map/all_gather | solution.py:16
  94.3 70.2 %all-gather.10.cloned.1.call-start = ((), (), s32[]{:S(2)}) async-start(), calls=%async_computation.4 | async-start | bytes 1310720 | tf_op jit(solution)/shard_map/all_gather | solution.py:15
  94.9 368.0 %all-gather.14.cloned.1.call-start = ((), (), s32[]{:S(2)}) async-start(), calls=%async_computation.6 | async-start | bytes 20971520 | tf_op jit(solution)/shard_map/all_gather | solution.py:51
  186.4 4.8 %copy-start.1 = (bf16[16,32,32,32]{3,2,0,1:T(8,128)(2,1)S(1)}, bf16[16,32,32,32]{3,2,0,1:T(8,128)(2,1)}, u32[]{:S(2)}) copy-start(bf16[16,32,32,32]{3,2,0,1:T(8,128)(2,1)} %copy.46) | copy-start | bytes 3145732
  304.1 2.2 copy-start.2
Sparse Core Ops, SparseCore 0:
  9.2 27.1 all-gather.5
  38.1 24.7 all-gather.7
  96.2 30.1 all-gather.11
  128.0 36.4 all-gather.9
  310.6 152.2 all-gather.13
where the time goes:
time: 483 us; the launch traced here: 482 us
  waiting for transfers between devices  255 us (53%)
  blocking collectives  105 us (22%)
  local copies, waits for them, and re-layouts  55.7 us (12%)
  matrix products  33.6 us (7%)
  starting transfers between devices  13.7 us (3%)
  between operations  13.2 us (3%)
  other arithmetic  5.23 us (1%)
    all_gather x1, waiting for transfers between devices, body(): lax.all_gather(gated, 'fsdp', axis=1, tiled=True)  152 us
    all_to_all x1, blocking collectives, body(): lax.all_to_all(outgoing, 'ctx', split_axis=0, concat_axis=1, tiled=True)  105 us
    all_gather x1, waiting for transfers between devices, body(): lax.all_gather(factor_a, 'fsdp', axis=0, tiled=True)  31.2 us
    all_gather x1, waiting for transfers between devices, body(): lax.all_gather(factor_d, 'fsdp', axis=0, tiled=True)  28.3 us
    all_gather x1, waiting for transfers between devices, body(): lax.all_gather(factor_b, 'fsdp', axis=0, tiled=True)  21.9 us
    reshape x2, local copies, waits for them, and re-layouts, body(): blocks_third.reshape(group_size, block_size, block_size, block_size)  16.3 us
    reshape x2, local copies, waits for them, and re-layouts, body(): blocks_last.reshape(group_size, block_size, block_size, block_size)  16.2 us
    all_to_all x1, starting transfers between devices, body(): lax.all_to_all(sectioned, 'ctx', split_axis=1, concat_axis=0, tiled=True)  13.4 us
  transfers between devices with their start and end apart: 6, of which 6 were waited for; matrix products, arithmetic and copies ran while one was open for 10% of the time, Pallas kernels for 0%

commit v1 on v0

v1 whole, which is shorter than its diff:
```python
import functools

import jax
import jax.numpy as jnp
from jax import lax
from jax.experimental import pallas as pl
from jax.experimental.pallas import tpu as pltpu
from jax.sharding import PartitionSpec as P

BLK = 32
LANES = 128
SUB = 8
WIDE = SUB * BLK
PACK = LANES // BLK
SQUARE = BLK * BLK
RANKS = 4
ALL = RANKS * LANES
BF16 = jnp.bfloat16
F32 = jnp.float32
VMEM_LIMIT = 44 * 1024 * 1024
RETURN_QUADS = (2, 1, 1)

VMEM = pl.BlockSpec(memory_space=pltpu.VMEM)
SMEM = pl.BlockSpec(memory_space=pltpu.SMEM)
ANY = pl.BlockSpec(memory_space=pl.ANY)
FACTOR = pltpu.VMEM((LANES, SQUARE), BF16)
WIDE_SHAPE = pltpu.VMEM((4, SUB, BLK, WIDE), BF16)
SPREAD_SHAPE = pltpu.VMEM((PACK, LANES, WIDE), BF16)


def call(kernel, name, out_shape, in_specs, out_specs, scratch, flops, moved, exps=0, aliases=None):
    return pl.pallas_call(
        kernel,
        name=name,
        out_shape=out_shape,
        in_specs=in_specs,
        out_specs=out_specs,
        scratch_shapes=scratch,
        input_output_aliases=aliases or {},
        compiler_params=pltpu.CompilerParams(vmem_limit_bytes=VMEM_LIMIT),
        cost_estimate=pl.CostEstimate(flops=flops, bytes_accessed=moved, transcendentals=exps),
    )


def aligned(start, size):
    return pl.ds(pl.multiple_of(start, size), size)


def started(copies):
    for copy in copies:
        copy.start()
    return copies


def finish(copies):
    for copy in copies:
        copy.wait()


def iota(shape, axis):
    return lax.broadcasted_iota(jnp.int32, shape, axis)


def ones_where(condition):
    return jnp.where(condition, 1.0, 0.0).astype(BF16)


def reorder(factor_ref, source_of):
    shape = (LANES, LANES)
    order = ones_where(source_of(iota(shape, 0)) == iota(shape, 1))
    factor_ref[...] = jnp.dot(order, factor_ref[...], preferred_element_type=F32).astype(BF16)


def widen_major(factor, wide_ref):
    rows = factor.astype(F32)
    block, row = iota((BLK, LANES), 1) // BLK, iota((BLK, LANES), 0) % SUB
    keeps = (block == row, block == row - PACK)
    for m in range(SUB):
        turned = rows[:, m * LANES : (m + 1) * LANES]
        rolled = [pltpu.roll(turned, turn * BLK, 1) for turn in range(1, PACK)]
        for turn in range(1, PACK):
            turned = jnp.where(row % PACK == turn, rolled[turn - 1], turned)
        for half in range(PACK // 2):
            parts = []
            for q in (2 * half, 2 * half + 1):
                here = turned if q == 0 else pltpu.roll(turned, LANES - q * BLK, 1)
                both = jnp.concatenate([jnp.where(keep, here, 0.0) for keep in keeps], axis=1)
                parts.append(both.reshape(4, SUB, WIDE))
            wide_ref[:, m, half * 16 : half * 16 + 16, :] = jnp.concatenate(parts, axis=1).astype(BF16)


def fill_spread(spread_ref):
    row, want = iota((LANES, WIDE), 0), iota((LANES, WIDE), 1) // 4 % BLK
    for q in range(PACK):
        spread_ref[q] = ones_where(row == want + q * BLK)


def widen_minor(factor, spread_ref, wide_ref):
    rows = factor.astype(F32).reshape(4, SUB, SQUARE)
    tiles = [rows[:, :, m * LANES : (m + 1) * LANES] for m in range(SUB)]
    left = jnp.stack(tiles, axis=1).reshape(WIDE, LANES).astype(BF16)
    shape = (1, SUB, WIDE)
    keep = iota(shape, 1) == iota(shape, 2) // LANES * 4 + iota(shape, 2) % 4
    for half in range(PACK // 2):
        parts = []
        for q in (2 * half, 2 * half + 1):
            part = jnp.dot(left, spread_ref[q], preferred_element_type=F32)
            parts.append(jnp.where(keep, part.reshape(BLK, SUB, WIDE), 0.0))
        both = jnp.concatenate(parts, axis=1).astype(BF16)
        wide_ref[:, :, half * 16 : half * 16 + 16, :] = both.reshape(4, SUB, 16, WIDE)


def apply(wide_ref, group, data):
    left = wide_ref[group].reshape(WIDE, WIDE)
    return jnp.dot(left, data, preferred_element_type=F32).reshape(BLK, SUB, data.shape[1])


def local_kernel(where_ref, tokens_ref, fd_ref, fc_ref, *rest):
    out_ref, tokens_v, fd_v, fc_v, wide_ref, first_ref, out_v, sem, out_sem = rest[-9:]
    quarter = where_ref[0]
    factors = started(
        [pltpu.make_async_copy(fd_ref, fd_v, sem.at[4]), pltpu.make_async_copy(fc_ref, fc_v, sem.at[5])]
    )
    arriving = started(
        [
            pltpu.make_async_copy(tokens_ref.at[aligned((quarter * 4 + p) * SQUARE, SQUARE), :], tokens_v.at[p], sem.at[p])
            for p in range(4)
        ]
    )
    finish(factors)
    reorder(fc_v, lambda r: r // 4 % 4 * BLK + r // 16 * 4 + r % 4)
    for p in range(4):
        widen_major(fd_v[p * BLK : (p + 1) * BLK, :], wide_ref)
        arriving[p].wait()
        for pair in range(2):
            halves = [
                apply(wide_ref, group, tokens_v[p, group * WIDE : (group + 1) * WIDE, :])
                for group in (2 * pair, 2 * pair + 1)
            ]
            first_ref[p, :, pair * 16 : pair * 16 + 16, :] = jnp.concatenate(halves, axis=1).astype(BF16)
    leaving = []
    for step in range(4):
        widen_major(fc_v[step * BLK : (step + 1) * BLK, :], wide_ref)
        for one in range(2):
            quad = 2 * step + one
            halves = []
            for pair in range(2):
                held = first_ref[2 * pair : 2 * pair + 2, 4 * quad : 4 * quad + 4]
                halves.append(apply(wide_ref, 2 * one + pair, held.reshape(WIDE, LANES)))
            out_v[quad] = jnp.concatenate(halves, axis=1).astype(BF16)
            target = out_ref.at[:, quad // 4, quad % 4, quarter]
            leaving += started([pltpu.make_async_copy(out_v.at[quad], target, out_sem.at[quad])])
    finish(leaving)


def local_steps(where, tokens, factor_d, factor_c, base):
    extra = [] if base is None else [base]
    return call(
        local_kernel,
        "steps_d_c",
        jax.ShapeDtypeStruct((BLK, 2, RANKS, RANKS, 16, LANES), BF16),
        [SMEM] + [ANY] * (3 + len(extra)),
        ANY,
        [
            pltpu.VMEM((4, SQUARE, LANES), BF16),
            FACTOR,
            FACTOR,
            WIDE_SHAPE,
            pltpu.VMEM((4, BLK, BLK, LANES), BF16),
            pltpu.VMEM((SUB, BLK, 16, LANES), BF16),
            pltpu.SemaphoreType.DMA((6,)),
            pltpu.SemaphoreType.DMA((SUB,)),
        ],
        flops=2**31,
        moved=3 * 2**20,
        aliases={4: 0} if extra else None,
    )(where, tokens, factor_d, factor_c, *extra)


def d_lo_minor(row):
    return row % 4 * BLK + row // 4


def step_a_quad(quad, third_ref, row_of, fa_v, spread_ref, wide_ref, sent_v, slot):
    rows = [fa_v[high * 64 + quad * 16 : high * 64 + quad * 16 + 16, :] for high in range(2)]
    widen_minor(jnp.concatenate(rows, axis=0), spread_ref, wide_ref)
    for high in range(2):
        halves = []
        for pair in range(2):
            first = row_of(high, quad) + 2 * pair
            halves.append(apply(wide_ref, 2 * high + pair, third_ref[first : first + 2].reshape(WIDE, ALL)))
        sent_v[slot, :, high] = jnp.concatenate(halves, axis=1).astype(BF16)


def middle_kernel(count, held_ref, fb_ref, fa_ref, *rest):
    third_ref, sent_ref, held_v, fb_v, fa_v, wide_ref, spread_ref, third_v, sent_v, sem, out_sem = rest[-11:]
    factors = started(
        [pltpu.make_async_copy(fb_ref, fb_v, sem.at[4]), pltpu.make_async_copy(fa_ref, fa_v, sem.at[5])]
    )
    arriving = started(
        [
            pltpu.make_async_copy(held_ref.at[pl.ds(8 * step, 8)], held_v.at[pl.ds(8 * step, 8)], sem.at[step])
            for step in range(4)
        ]
    )
    fill_spread(spread_ref)
    finish(factors)
    reorder(fb_v, d_lo_minor)
    reorder(fa_v, d_lo_minor)
    for step in range(4):
        widen_minor(fb_v[step * BLK : (step + 1) * BLK, :], spread_ref, wide_ref)
        arriving[step].wait()
        for quad in range(2):
            halves = []
            for pair in range(2):
                a = 8 * step + 4 * quad + 2 * pair
                data = [held_v[a : a + 2, :, rank].reshape(WIDE, LANES) for rank in range(RANKS)]
                halves.append(apply(wide_ref, 2 * quad + pair, jnp.concatenate(data, axis=1)))
            first = step * BLK + quad * 16
            third_v[:, first : first + 16, :] = jnp.concatenate(halves, axis=1).astype(BF16)
    later = 16 - 4 * count
    leaving = started(
        [
            pltpu.make_async_copy(
                third_v.at[pl.ds(high * 16 + 4 * count, later)],
                third_ref.at[pl.ds(high * 16 + 4 * count, later)],
                out_sem.at[high],
            )
            for high in range(2)
        ]
    )
    for quad in range(count):
        step_a_quad(quad, third_v, lambda high, at: high * 16 + at * 4, fa_v, spread_ref, wide_ref, sent_v, quad)
        leaving += started([pltpu.make_async_copy(sent_v.at[quad], sent_ref.at[:, :, quad], out_sem.at[2 + quad])])
    finish(leaving)


def sent_shape(count):
    return jax.ShapeDtypeStruct((BLK, 2, count, 16, ALL), BF16)


def middle(held, factor_b, factor_a, count, after):
    return call(
        functools.partial(middle_kernel, count),
        "steps_b_a",
        (jax.ShapeDtypeStruct((BLK, LANES, ALL), BF16), sent_shape(count)),
        [ANY] * (3 + len(after)),
        (ANY, ANY),
        [
            pltpu.VMEM(held.shape, BF16),
            FACTOR,
            FACTOR,
            WIDE_SHAPE,
            SPREAD_SHAPE,
            pltpu.VMEM((BLK, LANES, ALL), BF16),
            pltpu.VMEM((count, BLK, 2, 16, ALL), BF16),
            pltpu.SemaphoreType.DMA((6,)),
            pltpu.SemaphoreType.DMA((2 + count,)),
        ],
        flops=2**32,
        moved=9 * 2**20,
    )(held, factor_b, factor_a, *after)


def step_a_kernel(first_quad, count, third_ref, fa_ref, *rest):
    sent_ref, third_v, fa_v, wide_ref, spread_ref, sent_v, sem, out_sem = rest[-8:]
    arriving = started(
        [pltpu.make_async_copy(fa_ref, fa_v, sem.at[2])]
        + [
            pltpu.make_async_copy(
                third_ref.at[pl.ds(high * 16 + 4 * first_quad, 4 * count)],
                third_v.at[pl.ds(high * 4 * count, 4 * count)],
                sem.at[high],
            )
            for high in range(2)
        ]
    )
    fill_spread(spread_ref)
    finish(arriving)
    reorder(fa_v, d_lo_minor)
    leaving = []
    for slot in range(count):
        row_of = lambda high, quad: (high * count + quad - first_quad) * 4
        step_a_quad(first_quad + slot, third_v, row_of, fa_v, spread_ref, wide_ref, sent_v, slot)
        leaving += started([pltpu.make_async_copy(sent_v.at[slot], sent_ref.at[:, :, slot], out_sem.at[slot])])
    finish(leaving)


def step_a(third, factor_a, first_quad, count, after):
    return call(
        functools.partial(step_a_kernel, first_quad, count),
        "step_a",
        sent_shape(count),
        [ANY] * (2 + len(after)),
        ANY,
        [
            pltpu.VMEM((8 * count, LANES, ALL), BF16),
            FACTOR,
            WIDE_SHAPE,
            SPREAD_SHAPE,
            pltpu.VMEM((count, BLK, 2, 16, ALL), BF16),
            pltpu.SemaphoreType.DMA((3,)),
            pltpu.SemaphoreType.DMA((count,)),
        ],
        flops=2**29 * count,
        moved=2**21 * count,
    )(third, factor_a, *after)


def place_of(row, f):
    turn, s, p, low = row // 64, row // 16 % 4, row // 4 % 4, row % 4
    return p * 64 + s * 16 + (turn ^ f) * 4 + low


def split_kernel(f_ref, tokens_ref, w_ref, after_ref, *rest):
    out_refs, w_out_ref = rest[:RANKS], rest[RANKS]
    order_ref, tokens_v, out_v, sem, out_sem = rest[RANKS + 1 :]
    leaving = started([pltpu.make_async_copy(w_ref, w_out_ref, sem.at[4])])
    size = 4 * SQUARE
    arriving = started(
        [
            pltpu.make_async_copy(tokens_ref.at[pl.ds(quad * size, size), :], tokens_v.at[quad], sem.at[quad])
            for quad in range(4)
        ]
    )
    order_ref[...] = ones_where(place_of(iota((WIDE, WIDE), 0), f_ref[0]) == iota((WIDE, WIDE), 1))
    for quad in range(4):
        arriving[quad].wait()

        @pl.loop(0, 4)
        def _(step):
            blocks = []
            for one in range(4):
                rows = [tokens_v[quad, aligned(p * SQUARE + step * 256 + one * 64, 64), :] for p in range(4)]
                blocks.append(jnp.concatenate(rows, axis=0))
            held = jnp.concatenate(blocks, axis=1)
            moved = jnp.dot(order_ref[...], held, preferred_element_type=F32).astype(BF16)
            for turn in range(RANKS):
                for one in range(4):
                    block = moved[turn * 64 : turn * 64 + 64, one * LANES : (one + 1) * LANES]
                    out_v[turn, quad, aligned(step * 256 + one * 64, 64), :] = block

        leaving += started(
            [
                pltpu.make_async_copy(
                    out_v.at[turn, quad], out_refs[turn].at[pl.ds(quad * SQUARE, SQUARE), :], out_sem.at[turn, quad]
                )
                for turn in range(RANKS)
            ]
        )
    finish(leaving)


def split(f, tokens, w, after):
    quarter = jax.ShapeDtypeStruct((4 * SQUARE, LANES), BF16)
    *parts, w = call(
        split_kernel,
        "split",
        [quarter] * RANKS + [jax.ShapeDtypeStruct(w.shape, BF16)],
        [SMEM, ANY, ANY, ANY],
        [ANY] * (RANKS + 1),
        [
            pltpu.VMEM((WIDE, WIDE), BF16),
            pltpu.VMEM((4, 4 * SQUARE, LANES), BF16),
            pltpu.VMEM((RANKS, 4, SQUARE, LANES), BF16),
            pltpu.SemaphoreType.DMA((5,)),
            pltpu.SemaphoreType.DMA((RANKS, 4)),
        ],
        flops=2**30,
        moved=8 * 2**20,
    )(f, tokens, w, after)
    return parts, w


def project_kernel(first_quad, f_ref, mixed_ref, *rest):
    token_refs, w_refs, rest = rest[:RANKS], rest[RANKS : 2 * RANKS], rest[2 * RANKS :]
    out_refs = rest[-RANKS - 8 : -8]
    w_all_ref, w_v, mixed_v, tokens_v, out_v, w_sem, sem, out_sem = rest[-8:]
    f = f_ref[0]
    count = mixed_ref.shape[1]
    tile, steps = SQUARE // 4, 4 * count
    weights = started([pltpu.make_async_copy(w_refs[turn], w_v.at[turn], w_sem.at[turn]) for turn in range(RANKS)])
    arriving = []
    for step in range(steps):
        rows = pl.ds((first_quad * 4 + step) * tile, tile)
        source = mixed_ref.at[pl.ds(step % 4 * 16, 16), step // 4]
        arriving.append(
            started(
                [pltpu.make_async_copy(source, mixed_v.at[step], sem.at[step, RANKS])]
                + [
                    pltpu.make_async_copy(token_refs[turn].at[rows, :], tokens_v.at[turn, step], sem.at[step, turn])
                    for turn in range(RANKS)
                ]
            )
        )
    finish(weights)
    for row in range(RANKS):
        for column in range(RANKS):
            block = w_v[column, aligned((f ^ row) * LANES, LANES), :]
            w_all_ref[row * LANES : (row + 1) * LANES, column * LANES : (column + 1) * LANES] = block
    leaving = []
    for step in range(steps):
        finish(arriving[step])
        gated = []
        for turn in range(RANKS):
            mixed = mixed_v[step, :, :, aligned((f ^ turn) * LANES, LANES)].reshape(tile, LANES).astype(F32)
            value = tokens_v[turn, step].astype(F32)
            gated.append((mixed * (value / (1.0 + jnp.exp(-value)))).astype(BF16))
        result = jnp.dot(jnp.concatenate(gated, axis=1), w_all_ref[...], preferred_element_type=F32).astype(BF16)
        for turn in range(RANKS):
            out_v[turn, step] = result[:, turn * LANES : (turn + 1) * LANES]
            target = out_refs[turn].at[pl.ds(step * tile, tile), :]
            leaving += started([pltpu.make_async_copy(out_v.at[turn, step], target, out_sem.at[step, turn])])
    finish(leaving)


def project(f, mixed, tokens, w, first_quad, after):
    steps, tile = mixed.shape[1] * 4, SQUARE // 4
    size = steps * tile * ALL
    return call(
        functools.partial(project_kernel, first_quad),
        "project",
        [jax.ShapeDtypeStruct((steps * tile, LANES), BF16)] * RANKS,
        [SMEM] + [ANY] * (1 + 2 * RANKS + len(after)),
        [ANY] * RANKS,
        [
            pltpu.VMEM((ALL, ALL), BF16),
            pltpu.VMEM((RANKS, ALL, LANES), BF16),
            pltpu.VMEM((steps, 16, 16, ALL), BF16),
            pltpu.VMEM((RANKS, steps, tile, LANES), BF16),
            pltpu.VMEM((RANKS, steps, tile, LANES), BF16),
            pltpu.SemaphoreType.DMA((RANKS,)),
            pltpu.SemaphoreType.DMA((steps, RANKS + 1)),
            pltpu.SemaphoreType.DMA((steps, RANKS)),
        ],
        flops=size * 1024,
        moved=size * 6,
        exps=size,
    )(f, mixed, *tokens, *w, *after)


def merge_kernel(first_row, f_ref, *rest):
    part_refs, (out_ref, done_ref, order_ref, parts_v, held_v, sem, out_sem) = rest[:RANKS], rest[-7:]
    count = part_refs[0].shape[0] // SQUARE
    arriving = [
        started(
            [
                pltpu.make_async_copy(
                    part_refs[turn].at[pl.ds(quad * SQUARE, SQUARE), :], parts_v.at[turn, quad], sem.at[quad, turn]
                )
                for turn in range(RANKS)
            ]
        )
        for quad in range(count)
    ]
    done_ref[...] = jnp.zeros_like(done_ref)
    order_ref[...] = ones_where(place_of(iota((WIDE, WIDE), 1), f_ref[0]) == iota((WIDE, WIDE), 0))
    leaving = []
    for quad in range(count):
        finish(arriving[quad])

        @pl.loop(0, 4)
        def _(step):
            blocks = []
            for one in range(4):
                rows = [parts_v[turn, quad, aligned(step * 256 + one * 64, 64), :] for turn in range(RANKS)]
                blocks.append(jnp.concatenate(rows, axis=0))
            held = jnp.concatenate(blocks, axis=1)
            moved = jnp.dot(order_ref[...], held, preferred_element_type=F32).astype(BF16)
            for p in range(4):
                for one in range(4):
                    block = moved[p * 64 : p * 64 + 64, one * LANES : (one + 1) * LANES]
                    held_v[quad, aligned(p * SQUARE + step * 256 + one * 64, 64), :] = block

        rows = 4 * SQUARE
        target = out_ref.at[pl.ds(first_row + quad * rows, rows), :]
        leaving += started([pltpu.make_async_copy(held_v.at[quad], target, out_sem.at[quad])])
    finish(leaving)


def merge(f, parts, total, first_quad, base):
    rows = parts[0].shape[0]
    count = rows // SQUARE
    extra = [] if base is None else [base]
    return call(
        functools.partial(merge_kernel, first_quad * 4 * SQUARE),
        "merge",
        (jax.ShapeDtypeStruct((total, LANES), BF16), jax.ShapeDtypeStruct((SUB, LANES), F32)),
        [SMEM] + [ANY] * (RANKS + len(extra)),
        (ANY, VMEM),
        [
            pltpu.VMEM((WIDE, WIDE), BF16),
            pltpu.VMEM((RANKS, count, SQUARE, LANES), BF16),
            pltpu.VMEM((count, 4 * SQUARE, LANES), BF16),
            pltpu.SemaphoreType.DMA((count, RANKS)),
            pltpu.SemaphoreType.DMA((count,)),
        ],
        flops=rows * 4 * WIDE * LANES * 2,
        moved=rows * LANES * 16,
        aliases={5: 0} if extra else None,
    )(f, *parts, *extra)


TURNS = [[(rank, rank ^ turn) for rank in range(RANKS)] for turn in range(RANKS)]


def swap(parts):
    return [parts[0]] + [lax.ppermute(parts[turn], "fsdp", TURNS[turn]) for turn in (2, 1, 3)]


def in_turn(got):
    return [got[0], got[2], got[1], got[3]]


def share(x):
    chip = lax.ppermute(x, "fsdp", TURNS[2])
    core = lax.ppermute(x, "fsdp", TURNS[1])
    far = lax.ppermute(chip, "fsdp", TURNS[1])
    return [x, core, chip, far]


def body(tokens, factor_d, factor_c, factor_b, factor_a, w_proj):
    local_rows = tokens.shape[0]
    f = lax.axis_index("fsdp").astype(jnp.int32).reshape(1)

    flat = lambda factor: factor.reshape(-1, SQUARE)
    shared_d, shared_c = share(flat(factor_d)), share(flat(factor_c))

    second = None
    for turn in range(RANKS):
        second = local_steps(f ^ turn, tokens, shared_d[turn], shared_c[turn], second)
    token_parts, w = split(f, tokens, w_proj, second)
    token_parts = in_turn(swap(token_parts))
    w = share(w)
    arrived = lax.all_to_all(
        second.reshape(64 * RANKS, 64, LANES), ("ctx", "fsdp"), split_axis=0, concat_axis=0, tiled=True
    )
    weights_a = flat(factor_a)
    third, first_sent = middle(
        arrived.reshape(BLK, 2, RANKS, 64, LANES), flat(factor_b), weights_a, RETURN_QUADS[0], token_parts[1:] + w[1:]
    )

    out, first_quad = None, 0
    projected, ends = [], []
    for k, count in enumerate(RETURN_QUADS):
        if k == 0:
            sent = first_sent
        else:
            sent = step_a(third, weights_a, first_quad, count, projected[k - 2 : k - 1] if k >= 2 else [])
        mixed = lax.all_to_all(
            sent.reshape(64, count * 16, ALL), "ctx", split_axis=0, concat_axis=0, tiled=True
        ).reshape(64, count, 16, ALL)
        parts = project(f, mixed, token_parts, w, first_quad, ends[k - 2 : k - 1] if k >= 2 else [])
        out, done = merge(f, in_turn(swap(parts)), local_rows, first_quad, out)
        projected.append(parts[0])
        ends.append(done)
        first_quad += count
    return out


def solution(mesh):
    in_specs = (
        P("ctx", "fsdp"),
        P(("ctx", "fsdp"), None, None),
        P(("ctx", "fsdp"), None, None),
        P(("ctx", "fsdp"), None, None),
        P(("ctx", "fsdp"), None, None),
        P(None, "fsdp"),
    )
    out_specs = P("ctx", "fsdp")
    return jax.shard_map(body, mesh=mesh, in_specs=in_specs, out_specs=out_specs, check_vma=False)
```

time: 483 us -> 329 us (0.68)
  blocking collectives: 105 us -> 0 us
  waiting for transfers between devices: 255 us -> 180 us
  Pallas kernels: 0 us -> 56.4 us
  starting transfers between devices: 13.7 us -> 63.8 us
  matrix products: 33.6 us -> 0 us
  local copies, waits for them, and re-layouts: 55.7 us -> 23.1 us
  between operations: 13.2 us -> 0.82 us
  other arithmetic: 5.23 us -> 0 us
    all_gather x5 -> x0, waiting for transfers between devices: 247 us -> none  [the longest x1 152 us: body(): lax.all_gather(gated, 'fsdp', axis=1, tiled=True)]
    ppermute x0 -> x21, waiting for transfers between devices: none -> 120 us  [the longest x3 84.2 us: share(): chip = lax.ppermute(x, 'fsdp', TURNS[2])]
    all_to_all x1 -> x0, blocking collectives: 105 us -> none  [body(): lax.all_to_all(outgoing, 'ctx', split_axis=0, concat_axis=1, tiled=True)]
    pallas_call x0 -> x14, Pallas kernels: none -> 56.4 us  [the longest x3 17 us: project(): call(functools.partial(project_kernel, first_quad), 'project', [jax.Shape...]
    all_to_all x1 -> x4, waiting for transfers between devices: 5.61 us -> 59.5 us  [the longest x3 59.5 us: body(): lax.all_to_all(sent.reshape(64, count * 16, ALL), 'ctx', split_axis=0, co...]
    dot_general x5 -> x0, matrix products: 33.6 us -> none  [the longest x1 12.3 us: body(): jnp.dot(lax.all_gather(gated, 'fsdp', axis=1, tiled=True), w_proj, prefer...]
    reshape x5 -> x4, local copies, waits for them, and re-layouts: 35.7 us -> 5.05 us  [body(): flat = lambda factor: factor.reshape(-1, SQUARE)]
    all_to_all x1 -> x4, starting transfers between devices: 13.4 us -> 42.9 us  [the longest x3 27.5 us: body(): lax.all_to_all(sent.reshape(64, count * 16, ALL), 'ctx', split_axis=0, co...]
  transfers between devices with their start and end apart: 6 -> 25, of which waited for: 6 -> 8; matrix products, arithmetic and copies ran while one was open for 10% -> 1% of each run, Pallas kernels for 0% -> 14%
where the time goes in v1:
time: 329 us; the launch traced here: 324 us
  waiting for transfers between devices  180 us (55%)
  starting transfers between devices  63.8 us (19%)
  Pallas kernels  56.4 us (17%)
  local copies, waits for them, and re-layouts  23.1 us (7%)
    ppermute x3, waiting for transfers between devices, share(): chip = lax.ppermute(x, 'fsdp', TURNS[2])  84.2 us
    all_to_all x3, waiting for transfers between devices, body(): lax.all_to_all(sent.reshape(64, count * 16, ALL), 'ctx', split_axis=0, co...  59.5 us
    ppermute x12, waiting for transfers between devices, swap(): lax.ppermute(parts[turn], 'fsdp', TURNS[turn])  35.9 us
    all_to_all x3, starting transfers between devices, body(): lax.all_to_all(sent.reshape(64, count * 16, ALL), 'ctx', split_axis=0, co...  27.5 us
    unnamed x32, local copies, waits for them, and re-layouts  18 us
    pallas_call x3, Pallas kernels, project(): call(functools.partial(project_kernel, first_quad), 'project', [jax.Shape...  17 us
    pallas_call x4, Pallas kernels, local_steps(): call(local_kernel, 'steps_d_c', jax.ShapeDtypeStruct((BLK, 2, RANKS, RANK...  17 us
    all_to_all x1, starting transfers between devices, body(): lax.all_to_all(second.reshape(64 * RANKS, 64, LANES), ('ctx', 'fsdp'), sp...  15.4 us
  transfers between devices with their start and end apart: 25, of which 8 were waited for; matrix products, arithmetic and copies ran while one was open for 1% of the time, Pallas kernels for 14%

profile of v1, /device:TPU:1, one launch (start us, length us, event | category | flops | bytes accessed | tf_op | source)
XLA Modules:
  0.0 323.7 jit_solution(8591052138864771788)
XLA Ops:
  0.0 1.1 copy.17.fc_ref
  1.1 2.2 collective-permute-start.2
  3.3 1.1 copy.16.fd_ref
  4.5 3.1 collective-permute-start.5
  7.6 2.2 copy-done.1
  9.8 4.3 %steps_d_c.4.rest_0_ = bf16[32,2,4,4,16,128]{5,4,3,2,1,0:T(8,128)(2,1)S(1)} custom-call(s32[1]{0:T(128)} %bitcast.where_ref.f_ref, bf16[16384,128]{1,0:T(8,128)(2,1)S(1)} %copy-done.1, bf16[128,1024]{1,0:T(8,128)(2,1)S(1)} %copy.16.fd_ref, bf16[128,1024]{1,0:T(8,128)(2,1)S(1)} %copy.17.fc_ref), custom_call_target="tpu_custom_call" | custom-call | flops 2147483648 | bytes 3145728 | tf_op jit(solution)/shard_map/steps_d_c/pallas_call | solution.py:158
  14.7 1.7 collective-permute-start.1
  16.3 4.3 %steps_d_c.5.rest_0_ = bf16[32,2,4,4,16,128]{5,4,3,2,1,0:T(8,128)(2,1)S(1)} custom-call(s32[1]{0:T(128)S(6)} %xor.11.where_ref, bf16[16384,128]{1,0:T(8,128)(2,1)S(1)} %copy-done.1, bf16[128,1024]{1,0:T(8,128)(2,1)S(1)} %collective-permute-done.4.fd_ref, bf16[128,1024]{1,0:T(8,128)(2,1)S(1)} %collective-permute-done.5.fc_ref, ...), custom_call_target="tpu_custom_call", output_to_operand_aliasing={{}: (4, {})} | custom-call | flops 2147483648 | bytes 3145728 | tf_op jit(solution)/shard_map/steps_d_c/pallas_call | solution.py:158
  20.6 4.2 %steps_d_c.6.rest_0_ = bf16[32,2,4,4,16,128]{5,4,3,2,1,0:T(8,128)(2,1)S(1)} custom-call(s32[1]{0:T(128)S(6)} %xor.10.where_ref, bf16[16384,128]{1,0:T(8,128)(2,1)S(1)} %copy-done.1, bf16[128,1024]{1,0:T(8,128)(2,1)S(1)} %collective-permute-done.fd_ref, bf16[128,1024]{1,0:T(8,128)(2,1)S(1)} %collective-permute-done.2.fc_ref, ...), custom_call_target="tpu_custom_call", output_to_operand_aliasing={{}: (4, {})} | custom-call | flops 2147483648 | bytes 3145728 | tf_op jit(solution)/shard_map/steps_d_c/pallas_call | solution.py:158
  24.9 4.3 %steps_d_c.7.after_ref = bf16[32,2,4,4,16,128]{5,4,3,2,1,0:T(8,128)(2,1)S(1)} custom-call(s32[1]{0:T(128)S(6)} %xor.9.where_ref, bf16[16384,128]{1,0:T(8,128)(2,1)S(1)} %copy-done.1, bf16[128,1024]{1,0:T(8,128)(2,1)S(1)} %collective-permute-done.1.fd_ref, bf16[128,1024]{1,0:T(8,128)(2,1)S(1)} %collective-permute-done.3.fc_ref, ...), custom_call_target="tpu_custom_call", output_to_operand_aliasing={{}: (4, {})} | custom-call | flops 2147483648 | bytes 3145728 | tf_op jit(solution)/shard_map/steps_d_c/pallas_call | solution.py:158
  29.2 2.0 copy-done
  31.2 15.4 %all-to-all-start = ((bf16[256,64,128]{2,1,0:T(8,128)(2,1)}), bf16[256,64,128]{2,1,0:T(8,128)(2,1)}, u32[]{:S(2)}, u32[]{:S(2)}) async-start(bf16[256,64,128]{2,1,0:T(8,128)(2,1)} %bitcast.13), calls=%async_computation | async-start | bytes 8388608 | tf_op jit(solution)/shard_map/all_to_all | solution.py:535
  46.6 2.2 copy-done.2
  48.8 5.4 %split.1 = (bf16[4096,128]{1,0:T(8,128)(2,1)S(1)}, bf16[4096,128]{1,0:T(8,128)(2,1)}, bf16[4096,128]{1,0:T(8,128)(2,1)}, bf16[4096,128]{1,0:T(8,128)(2,1)}, bf16[512,128]{1,0:T(8,128)(2,1)S(1)}) custom-call(s32[1]{0:T(128)} %bitcast.where_ref.f_ref, bf16[16384,128]{1,0:T(8,128)(2,1)S(1)} %copy-done.2, bf16[512,128]{1,0:T(8,128)(2,1)S(1)} %copy-done.12, ...), custom_call_target="tpu_custom_call" | custom-call | flops 1073741824 | bytes 8388608 | tf_op jit(solution)/shard_map/split/pallas_call | solution.py:356
  54.3 2.3 collective-permute-start.6
  56.6 1.7 collective-permute-start.8
  58.9 84.1 %collective-permute-done.10.rest_4_.rest_6_ = bf16[512,128]{1,0:T(8,128)(2,1)} collective-permute-done((bf16[512,128]{1,0:T(8,128)(2,1)S(1)}, bf16[512,128]{1,0:T(8,128)(2,1)}, u32[]{:S(2)}, u32[]{:S(2)}) %collective-permute-start.10) | collective-permute-done | bytes 131104 | tf_op jit(solution)/shard_map/ppermute | solution.py:516
  143.6 1.1 copy.23.fa_ref
  144.7 1.8 copy.22.fb_ref
  147.5 5.3 %steps_b_a.1 = (bf16[32,128,512]{2,1,0:T(8,128)(2,1)S(1)}, bf16[32,2,2,16,512]{4,3,2,1,0:T(8,128)(2,1)S(1)}) custom-call(bf16[32,2,4,64,128]{4,3,2,1,0:T(8,128)(2,1)} %bitcast.4.held_ref, bf16[128,1024]{1,0:T(8,128)(2,1)S(1)} %copy-done.11, bf16[128,1024]{1,0:T(8,128)(2,1)S(1)} %copy.23.fa_ref, bf16[4096,128]{1,0:T(8,128)(2,1)S(1)} %collective-permute-done.6.rest_0_.rest_1_, ...), custom_call_target="tpu_custom_call" | custom-call | flops 4294967296 | bytes 9437184 | tf_op jit(solution)/shard_map/steps_b_a/pallas_call | solution.py:243
  152.8 2.0 copy-done.3
  154.8 1.3 copy-done.10
  156.2 9.8 %all-to-all-start.1 = ((bf16[64,32,512]{2,1,0:T(8,128)(2,1)}), bf16[64,32,512]{2,1,0:T(8,128)(2,1)}, u32[]{:S(2)}, u32[]{:S(2)}) async-start(bf16[64,32,512]{2,1,0:T(8,128)(2,1)} %bitcast.16), calls=%async_computation.1 | async-start | bytes 4194304 | tf_op jit(solution)/shard_map/all_to_all | solution.py:550
  166.0 2.2 copy-done.4
  168.1 1.1 step_a.3
  169.2 1.0 copy-done.7
  170.2 45.5 %all-to-all-done.1 = bf16[64,32,512]{2,1,0:T(8,128)(2,1)} async-done(((bf16[64,32,512]{2,1,0:T(8,128)(2,1)}), bf16[64,32,512]{2,1,0:T(8,128)(2,1)}, u32[]{:S(2)}, u32[]{:S(2)}) %all-to-all-start.1) | async-done | bytes 2097184 | tf_op jit(solution)/shard_map/all_to_all | solution.py:550
  215.6 9.5 %all-to-all-start.3 = ((bf16[64,16,512]{2,1,0:T(8,128)(2,1)}), bf16[64,16,512]{2,1,0:T(8,128)(2,1)}, u32[]{:S(2)}, u32[]{:S(2)}) async-start(bf16[64,16,512]{2,1,0:T(8,128)(2,1)} %bitcast.15), calls=%async_computation.3 | async-start | bytes 2097152 | tf_op jit(solution)/shard_map/all_to_all | solution.py:550
  225.2 8.6 %project.3 = (bf16[2048,128]{1,0:T(8,128)(2,1)S(1)}, bf16[2048,128]{1,0:T(8,128)(2,1)S(1)}, bf16[2048,128]{1,0:T(8,128)(2,1)S(1)}, bf16[2048,128]{1,0:T(8,128)(2,1)S(1)}) custom-call(s32[1]{0:T(128)} %bitcast.where_ref.f_ref, bf16[64,2,16,512]{3,2,1,0:T(8,128)(2,1)} %bitcast.8.mixed_ref, bf16[4096,128]{1,0:T(8,128)(2,1)S(1)} %get-tuple-element.34.rest_0_, ...), custom_call_target="tpu_custom_call" | custom-call | flops 1073741824 | bytes 6291456 | tf_op jit(solution)/shard_map/project/pallas_call | solution.py:420
  236.2 1.1 step_a.2
  237.2 1.0 copy-done.6
  239.0 14.0 %all-to-all-done.3 = bf16[64,16,512]{2,1,0:T(8,128)(2,1)} async-done(((bf16[64,16,512]{2,1,0:T(8,128)(2,1)}), bf16[64,16,512]{2,1,0:T(8,128)(2,1)}, u32[]{:S(2)}, u32[]{:S(2)}) %all-to-all-start.3) | async-done | bytes 1048608 | tf_op jit(solution)/shard_map/all_to_all | solution.py:550
  253.0 8.2 %all-to-all-start.2 = ((bf16[64,16,512]{2,1,0:T(8,128)(2,1)}), bf16[64,16,512]{2,1,0:T(8,128)(2,1)}, u32[]{:S(2)}, u32[]{:S(2)}) async-start(bf16[64,16,512]{2,1,0:T(8,128)(2,1)} %bitcast.14), calls=%async_computation.2 | async-start | bytes 2097152 | tf_op jit(solution)/shard_map/all_to_all | solution.py:550
  261.3 1.8 collective-permute-start.12
  263.4 1.4 collective-permute-start.14
  264.8 4.0 %project.5 = (bf16[1024,128]{1,0:T(8,128)(2,1)S(1)}, bf16[1024,128]{1,0:T(8,128)(2,1)}, bf16[1024,128]{1,0:T(8,128)(2,1)}, bf16[1024,128]{1,0:T(8,128)(2,1)}) custom-call(s32[1]{0:T(128)} %bitcast.where_ref.f_ref, bf16[64,1,16,512]{3,2,1,0:T(8,128)(2,1)} %bitcast.12.mixed_ref, bf16[4096,128]{1,0:T(8,128)(2,1)S(1)} %get-tuple-element.34.rest_0_, ...), custom_call_target="tpu_custom_call" | custom-call | flops 536870912 | bytes 3145728 | tf_op jit(solution)/shard_map/project/pallas_call | solution.py:420
  269.4 1.7 collective-permute-start.20
  271.1 14.8 %collective-permute-done.13.rest_2_ = bf16[2048,128]{1,0:T(8,128)(2,1)S(1)} collective-permute-done((bf16[2048,128]{1,0:T(8,128)(2,1)}, bf16[2048,128]{1,0:T(8,128)(2,1)S(1)}, u32[]{:S(2)}, u32[]{:S(2)}) %collective-permute-start.13) | collective-permute-done | bytes 524320 | tf_op jit(solution)/shard_map/ppermute | solution.py:508
  285.9 12.6 %collective-permute-done.14.rest_3_ = bf16[2048,128]{1,0:T(8,128)(2,1)S(1)} collective-permute-done((bf16[2048,128]{1,0:T(8,128)(2,1)}, bf16[2048,128]{1,0:T(8,128)(2,1)S(1)}, u32[]{:S(2)}, u32[]{:S(2)}) %collective-permute-start.14) | collective-permute-done | bytes 524320 | tf_op jit(solution)/shard_map/ppermute | solution.py:508
  298.4 3.1 merge.3
  301.6 4.5 %project.4 = (bf16[1024,128]{1,0:T(8,128)(2,1)S(1)}, bf16[1024,128]{1,0:T(8,128)(2,1)S(1)}, bf16[1024,128]{1,0:T(8,128)(2,1)S(1)}, bf16[1024,128]{1,0:T(8,128)(2,1)S(1)}) custom-call(s32[1]{0:T(128)} %bitcast.where_ref.f_ref, bf16[64,1,16,512]{3,2,1,0:T(8,128)(2,1)} %bitcast.10.mixed_ref, bf16[4096,128]{1,0:T(8,128)(2,1)S(1)} %get-tuple-element.34.rest_0_, ...), custom_call_target="tpu_custom_call" | custom-call | flops 536870912 | bytes 3145728 | tf_op jit(solution)/shard_map/project/pallas_call | solution.py:420
  306.1 1.1 collective-permute-start.16
  307.3 1.0 collective-permute-start.17
  308.3 1.5 collective-permute-done.20.rest_3_
  309.8 3.7 %merge.4 = (bf16[16384,128]{1,0:T(8,128)(2,1)}, f32[8,128]{1,0:T(8,128)}) custom-call(s32[1]{0:T(128)} %bitcast.where_ref.f_ref, bf16[1024,128]{1,0:T(8,128)(2,1)S(1)} %get-tuple-element.44.rest_0_, bf16[1024,128]{1,0:T(8,128)(2,1)} %collective-permute-done.18.rest_1_, ...), custom_call_target="tpu_custom_call", output_to_operand_aliasing={{0}: (5, {})} | custom-call | flops 268435456 | bytes 2097152 | tf_op jit(solution)/shard_map/merge/pallas_call | solution.py:485
  313.5 1.4 collective-permute-done.16.rest_2_
  314.8 5.7 %collective-permute-done.17.rest_3_ = bf16[1024,128]{1,0:T(8,128)(2,1)S(1)} collective-permute-done((bf16[1024,128]{1,0:T(8,128)(2,1)S(1)}, bf16[1024,128]{1,0:T(8,128)(2,1)S(1)}, u32[]{:S(2)}, u32[]{:S(2)}) %collective-permute-start.17) | collective-permute-done | bytes 262176 | tf_op jit(solution)/shard_map/ppermute | solution.py:508
  320.5 2.7 merge.5
  (52 shorter events, 7.0 us)
Async XLA Ops:
  1.1 13.0 %collective-permute-start.2 = (bf16[128,1024]{1,0:T(8,128)(2,1)S(1)}, bf16[128,1024]{1,0:T(8,128)(2,1)S(1)}, u32[]{:S(2)}, u32[]{:S(2)}) collective-permute-start(bf16[128,1024]{1,0:T(8,128)(2,1)S(1)} %copy.17.fc_ref), channel_id=1, source_target_pairs={{0,2},{1,3},{2,0},{3,1},{4,6},{5,7},{6,4},{7,5},{8,10},{9,11},{10,... | collective-permute-start | bytes 786440 | tf_op jit(solution)/shard_map/ppermute | solution.py:516
  4.4 10.3 %collective-permute-start = (bf16[128,1024]{1,0:T(8,128)(2,1)S(1)}, bf16[128,1024]{1,0:T(8,128)(2,1)S(1)}, u32[]{:S(2)}, u32[]{:S(2)}) collective-permute-start(bf16[128,1024]{1,0:T(8,128)(2,1)S(1)} %copy.16.fd_ref), channel_id=1, source_target_pairs={{0,2},{1,3},{2,0},{3,1},{4,6},{5,7},{6,4},{7,5},{8,10},{9,11},{10,... | collective-permute-start | bytes 786440 | tf_op jit(solution)/shard_map/ppermute | solution.py:516
  4.5 11.8 %collective-permute-start.5 = (bf16[128,1024]{1,0:T(8,128)(2,1)S(1)}, bf16[128,1024]{1,0:T(8,128)(2,1)S(1)}, u32[]{:S(2)}, u32[]{:S(2)}) collective-permute-start(bf16[128,1024]{1,0:T(8,128)(2,1)S(1)} %copy.17.fc_ref), channel_id=1, source_target_pairs={{0,1},{1,0},{2,3},{3,2},{4,5},{5,4},{6,7},{7,6},{8,9},{9,8},{10,11... | collective-permute-start | bytes 786440 | tf_op jit(solution)/shard_map/ppermute | solution.py:517
  7.6 8.7 %collective-permute-start.4 = (bf16[128,1024]{1,0:T(8,128)(2,1)S(1)}, bf16[128,1024]{1,0:T(8,128)(2,1)S(1)}, u32[]{:S(2)}, u32[]{:S(2)}) collective-permute-start(bf16[128,1024]{1,0:T(8,128)(2,1)S(1)} %copy.16.fd_ref), channel_id=1, source_target_pairs={{0,1},{1,0},{2,3},{3,2},{4,5},{5,4},{6,7},{7,6},{8,9},{9,8},{10,11... | collective-permute-start | bytes 786440 | tf_op jit(solution)/shard_map/ppermute | solution.py:517
  7.6 2.2 copy-start.1
  14.1 10.8 %collective-permute-start.3 = (bf16[128,1024]{1,0:T(8,128)(2,1)S(1)}, bf16[128,1024]{1,0:T(8,128)(2,1)S(1)}, u32[]{:S(2)}, u32[]{:S(2)}) collective-permute-start(bf16[128,1024]{1,0:T(8,128)(2,1)S(1)} %collective-permute-done.2.fc_ref), channel_id=1, source_target_pairs={{0,1},{1,0},{2,3},{3,2},{4,5},{5,4},{6,7},{7,6},{8,9},{9,8},{10,11... | collective-permute-start | bytes 786440 | tf_op jit(solution)/shard_map/ppermute | solution.py:518
  14.7 10.2 %collective-permute-start.1 = (bf16[128,1024]{1,0:T(8,128)(2,1)S(1)}, bf16[128,1024]{1,0:T(8,128)(2,1)S(1)}, u32[]{:S(2)}, u32[]{:S(2)}) collective-permute-start(bf16[128,1024]{1,0:T(8,128)(2,1)S(1)} %collective-permute-done.fd_ref), channel_id=1, source_target_pairs={{0,1},{1,0},{2,3},{3,2},{4,5},{5,4},{6,7},{7,6},{8,9},{9,8},{10,11... | collective-permute-start | bytes 786440 | tf_op jit(solution)/shard_map/ppermute | solution.py:518
  29.2 2.0 copy-start
  31.2 15.4 %copy-start.12 = (bf16[512,128]{1,0:T(8,128)(2,1)S(1)}, bf16[512,128]{1,0:T(8,128)(2,1)}, u32[]{:S(2)}) copy-start(bf16[512,128]{1,0:T(8,128)(2,1)} %w_ref.1) | copy-start | bytes 393220
  31.2 115.3 %all-to-all-start = ((bf16[256,64,128]{2,1,0:T(8,128)(2,1)}), bf16[256,64,128]{2,1,0:T(8,128)(2,1)}, u32[]{:S(2)}, u32[]{:S(2)}) async-start(bf16[256,64,128]{2,1,0:T(8,128)(2,1)} %bitcast.13), calls=%async_computation | async-start | bytes 8388608 | tf_op jit(solution)/shard_map/all_to_all | solution.py:535
  46.6 2.2 copy-start.2
  54.3 92.2 %collective-permute-start.6 = (bf16[4096,128]{1,0:T(8,128)(2,1)}, bf16[4096,128]{1,0:T(8,128)(2,1)S(1)}, u32[]{:S(2)}, u32[]{:S(2)}) collective-permute-start(bf16[4096,128]{1,0:T(8,128)(2,1)} %get-tuple-element.28), channel_id=1, source_target_pairs={{0,1},{1,0},{2,3},{3,2},{4,5},{5,4},{6,7},{7,6},{8,9},{9,8},{10,11... | collective-permute-start | bytes 3145736 | tf_op jit(solution)/shard_map/ppermute | solution.py:508
  56.6 89.9 %collective-permute-start.7 = (bf16[4096,128]{1,0:T(8,128)(2,1)}, bf16[4096,128]{1,0:T(8,128)(2,1)S(1)}, u32[]{:S(2)}, u32[]{:S(2)}) collective-permute-start(bf16[4096,128]{1,0:T(8,128)(2,1)} %get-tuple-element.29), channel_id=1, source_target_pairs={{0,2},{1,3},{2,0},{3,1},{4,6},{5,7},{6,4},{7,5},{8,10},{9,11},{10,... | collective-permute-start | bytes 3145736 | tf_op jit(solution)/shard_map/ppermute | solution.py:508
  56.6 89.9 %collective-permute-start.8 = (bf16[4096,128]{1,0:T(8,128)(2,1)}, bf16[4096,128]{1,0:T(8,128)(2,1)}, u32[]{:S(2)}, u32[]{:S(2)}) collective-permute-start(bf16[4096,128]{1,0:T(8,128)(2,1)} %get-tuple-element.30), channel_id=1, source_target_pairs={{0,3},{1,2},{2,1},{3,0},{4,7},{5,6},{6,5},{7,4},{8,11},{9,10},{10,... | collective-permute-start | bytes 3145736 | tf_op jit(solution)/shard_map/ppermute | solution.py:508
  58.3 84.8 %collective-permute-start.10 = (bf16[512,128]{1,0:T(8,128)(2,1)S(1)}, bf16[512,128]{1,0:T(8,128)(2,1)}, u32[]{:S(2)}, u32[]{:S(2)}) collective-permute-start(bf16[512,128]{1,0:T(8,128)(2,1)S(1)} %get-tuple-element.31.rest_4_), channel_id=1, source_target_pairs={{0,2},{1,3},{2,0},{3,1},{4,6},{5,7},{6,4},{7,5},{8,10},{9,11},{10,... | collective-permute-start | bytes 393224 | tf_op jit(solution)/shard_map/ppermute | solution.py:516
  58.5 88.0 %collective-permute-start.9 = (bf16[512,128]{1,0:T(8,128)(2,1)S(1)}, bf16[512,128]{1,0:T(8,128)(2,1)}, u32[]{:S(2)}, u32[]{:S(2)}) collective-permute-start(bf16[512,128]{1,0:T(8,128)(2,1)S(1)} %get-tuple-element.31.rest_4_), channel_id=1, source_target_pairs={{0,1},{1,0},{2,3},{3,2},{4,5},{5,4},{6,7},{7,6},{8,9},{9,8},{10,11... | collective-permute-start | bytes 393224 | tf_op jit(solution)/shard_map/ppermute | solution.py:517
  143.1 3.4 %collective-permute-start.11 = (bf16[512,128]{1,0:T(8,128)(2,1)}, bf16[512,128]{1,0:T(8,128)(2,1)}, u32[]{:S(2)}, u32[]{:S(2)}) collective-permute-start(bf16[512,128]{1,0:T(8,128)(2,1)} %collective-permute-done.10.rest_4_.rest_6_), channel_id=1, source_target_pairs={{0,1},{1,0},{2,3},{3,2},{4,5},{5,4},{6,7},{7,6},{8,9},{9,8},{10,11... | collective-permute-start | bytes 393224 | tf_op jit(solution)/shard_map/ppermute | solution.py:518
  146.5 1.0 copy-start.11
  152.8 2.0 copy-start.3
  154.8 1.3 copy-start.10
  156.2 59.5 %all-to-all-start.1 = ((bf16[64,32,512]{2,1,0:T(8,128)(2,1)}), bf16[64,32,512]{2,1,0:T(8,128)(2,1)}, u32[]{:S(2)}, u32[]{:S(2)}) async-start(bf16[64,32,512]{2,1,0:T(8,128)(2,1)} %bitcast.16), calls=%async_computation.1 | async-start | bytes 4194304 | tf_op jit(solution)/shard_map/all_to_all | solution.py:550
  165.9 2.2 copy-start.4
  169.2 1.0 copy-start.7
  215.6 37.4 %all-to-all-start.3 = ((bf16[64,16,512]{2,1,0:T(8,128)(2,1)}), bf16[64,16,512]{2,1,0:T(8,128)(2,1)}, u32[]{:S(2)}, u32[]{:S(2)}) async-start(bf16[64,16,512]{2,1,0:T(8,128)(2,1)} %bitcast.15), calls=%async_computation.3 | async-start | bytes 2097152 | tf_op jit(solution)/shard_map/all_to_all | solution.py:550
  225.2 11.0 %copy-start.5 = (bf16[32,128,512]{2,1,0:T(8,128)(2,1)S(1)}, bf16[32,128,512]{2,1,0:T(8,128)(2,1)}, u32[]{:S(2)}) copy-start(bf16[32,128,512]{2,1,0:T(8,128)(2,1)} %copy-done.3) | copy-start | bytes 12582916
  233.8 0.8 copy-start.13
  234.5 0.8 copy-start.14
  235.4 0.8 copy-start.15
  237.2 1.0 copy-start.6
  238.2 0.8 copy-start.8
  253.0 48.5 %all-to-all-start.2 = ((bf16[64,16,512]{2,1,0:T(8,128)(2,1)}), bf16[64,16,512]{2,1,0:T(8,128)(2,1)}, u32[]{:S(2)}, u32[]{:S(2)}) async-start(bf16[64,16,512]{2,1,0:T(8,128)(2,1)} %bitcast.14), calls=%async_computation.2 | async-start | bytes 2097152 | tf_op jit(solution)/shard_map/all_to_all | solution.py:550
  261.2 37.2 %copy-start.9 = (bf16[2048,128]{1,0:T(8,128)(2,1)S(1)}, bf16[2048,128]{1,0:T(8,128)(2,1)}, u32[]{:S(2)}) copy-start(bf16[2048,128]{1,0:T(8,128)(2,1)} %copy-done.8) | copy-start | bytes 1572868
  261.3 8.1 %collective-permute-start.12 = (bf16[2048,128]{1,0:T(8,128)(2,1)}, bf16[2048,128]{1,0:T(8,128)(2,1)S(1)}, u32[]{:S(2)}, u32[]{:S(2)}) collective-permute-start(bf16[2048,128]{1,0:T(8,128)(2,1)} %copy-done.15), channel_id=1, source_target_pairs={{0,1},{1,0},{2,3},{3,2},{4,5},{5,4},{6,7},{7,6},{8,9},{9,8},{10,11... | collective-permute-start | bytes 1572872 | tf_op jit(solution)/shard_map/ppermute | solution.py:508
  263.1 22.8 %collective-permute-start.13 = (bf16[2048,128]{1,0:T(8,128)(2,1)}, bf16[2048,128]{1,0:T(8,128)(2,1)S(1)}, u32[]{:S(2)}, u32[]{:S(2)}) collective-permute-start(bf16[2048,128]{1,0:T(8,128)(2,1)} %copy-done.14), channel_id=1, source_target_pairs={{0,2},{1,3},{2,0},{3,1},{4,6},{5,7},{6,4},{7,5},{8,10},{9,11},{10,... | collective-permute-start | bytes 1572872 | tf_op jit(solution)/shard_map/ppermute | solution.py:508
  263.4 35.0 %collective-permute-start.14 = (bf16[2048,128]{1,0:T(8,128)(2,1)}, bf16[2048,128]{1,0:T(8,128)(2,1)S(1)}, u32[]{:S(2)}, u32[]{:S(2)}) collective-permute-start(bf16[2048,128]{1,0:T(8,128)(2,1)} %copy-done.13), channel_id=1, source_target_pairs={{0,3},{1,2},{2,1},{3,0},{4,7},{5,6},{6,5},{7,4},{8,11},{9,10},{10,... | collective-permute-start | bytes 1572872 | tf_op jit(solution)/shard_map/ppermute | solution.py:508
  268.8 38.4 %collective-permute-start.18 = (bf16[1024,128]{1,0:T(8,128)(2,1)}, bf16[1024,128]{1,0:T(8,128)(2,1)}, u32[]{:S(2)}, u32[]{:S(2)}) collective-permute-start(bf16[1024,128]{1,0:T(8,128)(2,1)} %get-tuple-element.45), channel_id=1, source_target_pairs={{0,1},{1,0},{2,3},{3,2},{4,5},{5,4},{6,7},{7,6},{8,9},{9,8},{10,11... | collective-permute-start | bytes 786440 | tf_op jit(solution)/shard_map/ppermute | solution.py:508
  269.1 39.2 %collective-permute-start.19 = (bf16[1024,128]{1,0:T(8,128)(2,1)}, bf16[1024,128]{1,0:T(8,128)(2,1)}, u32[]{:S(2)}, u32[]{:S(2)}) collective-permute-start(bf16[1024,128]{1,0:T(8,128)(2,1)} %get-tuple-element.46), channel_id=1, source_target_pairs={{0,2},{1,3},{2,0},{3,1},{4,6},{5,7},{6,4},{7,5},{8,10},{9,11},{10,... | collective-permute-start | bytes 786440 | tf_op jit(solution)/shard_map/ppermute | solution.py:508
  269.4 40.4 %collective-permute-start.20 = (bf16[1024,128]{1,0:T(8,128)(2,1)}, bf16[1024,128]{1,0:T(8,128)(2,1)}, u32[]{:S(2)}, u32[]{:S(2)}) collective-permute-start(bf16[1024,128]{1,0:T(8,128)(2,1)} %get-tuple-element.47), channel_id=1, source_target_pairs={{0,3},{1,2},{2,1},{3,0},{4,7},{5,6},{6,5},{7,4},{8,11},{9,10},{10,... | collective-permute-start | bytes 786440 | tf_op jit(solution)/shard_map/ppermute | solution.py:508
  306.0 7.4 %collective-permute-start.15 = (bf16[1024,128]{1,0:T(8,128)(2,1)S(1)}, bf16[1024,128]{1,0:T(8,128)(2,1)S(1)}, u32[]{:S(2)}, u32[]{:S(2)}) collective-permute-start(bf16[1024,128]{1,0:T(8,128)(2,1)S(1)} %get-tuple-element.41), channel_id=1, source_target_pairs={{0,1},{1,0},{2,3},{3,2},{4,5},{5,4},{6,7},{7,6},{8,9},{9,8},{10,11... | collective-permute-start | bytes 786440 | tf_op jit(solution)/shard_map/ppermute | solution.py:508
  306.1 8.7 %collective-permute-start.16 = (bf16[1024,128]{1,0:T(8,128)(2,1)S(1)}, bf16[1024,128]{1,0:T(8,128)(2,1)S(1)}, u32[]{:S(2)}, u32[]{:S(2)}) collective-permute-start(bf16[1024,128]{1,0:T(8,128)(2,1)S(1)} %get-tuple-element.42), channel_id=1, source_target_pairs={{0,2},{1,3},{2,0},{3,1},{4,6},{5,7},{6,4},{7,5},{8,10},{9,11},{10,... | collective-permute-start | bytes 786440 | tf_op jit(solution)/shard_map/ppermute | solution.py:508
  307.3 13.3 %collective-permute-start.17 = (bf16[1024,128]{1,0:T(8,128)(2,1)S(1)}, bf16[1024,128]{1,0:T(8,128)(2,1)S(1)}, u32[]{:S(2)}, u32[]{:S(2)}) collective-permute-start(bf16[1024,128]{1,0:T(8,128)(2,1)S(1)} %get-tuple-element.43), channel_id=1, source_target_pairs={{0,3},{1,2},{2,1},{3,0},{4,7},{5,6},{6,5},{7,4},{8,11},{9,10},{10,... | collective-permute-start | bytes 786440 | tf_op jit(solution)/shard_map/ppermute | solution.py:508
